TPU v7x, 256 devices: a whole 4x4x8 slice. The times are simulated.
256 devices in a mesh: layer: 64 (over z, y, x_lo), row: 2 (over x_hi), col: 2 (over core).
Axes of the slice: x: 4 (x_hi: 2, x_lo: 2; x = x_hi * 2 + x_lo), y: 4, z: 8, core: 2. Of those that a mesh axis runs over, the one named last changes fastest.
Arguments:
- markov: bfloat16 [16384, 16384], P('row', ('layer', 'col')), may hold values from 0.049804688 to 1
- markov_tiles: int32 [256, 256], P('row', ('layer', 'col')), may hold values from 0 to 1, as said below
- slab: bfloat16 [16384, 2048], P(('layer', 'row'), 'col'), may hold values from 0.049804688 to 1
- slab_tiles: int32 [256, 32], P(('layer', 'row'), 'col'), may hold values from 0 to 1, as said below
Outputs:
- inflated: float32 [16384, 2048], P(('row', 'layer'), 'col')
Inputs may be any that keep to these rules, and one draw needn't show every extreme that they name: `markov_tiles`: every diagonal tile of the network matrix is present. `slab_tiles`: tile (c, c) of the slab is present for every slab tile column c.
All inputs are finite; a program needn't handle non-finite values.
Results may differ from a plain program's by a relative error of at most 0.0003.
Values may be sent and summed in bfloat16 or wider, within the bound.
No kernel may reach another device: no remote copies, remote signals or barrier semaphores. Data moves between devices by JAX's collectives and lax.ppermute only.
A program may use at most 128 MiB of HBM per device.

v0:
```python
import jax
import jax.numpy as jnp
from jax import lax
from jax.sharding import PartitionSpec as P


def widen(pattern, tile):
    rows, cols = pattern.shape
    ones = pattern.astype(jnp.bfloat16)
    return jnp.broadcast_to(ones[:, None, :, None], (rows, tile, cols, tile)).reshape(
        rows * tile, cols * tile
    )


def per_device(markov, markov_tiles, slab, slab_tiles):
    tile_size = markov.shape[0] // markov_tiles.shape[0]
    left = markov * widen(markov_tiles, tile_size)
    right = slab * widen(slab_tiles, tile_size)
    total_rows = left.shape[0] * lax.axis_size("row")
    inner = lax.all_gather(right, "row", axis=0, tiled=True)
    partial_value = jnp.dot(
        lax.all_gather(left, "col", axis=1, tiled=True), inner, preferred_element_type=jnp.float32
    )
    owned = lax.psum_scatter(partial_value, "layer", scatter_dimension=0, tiled=True)
    squared = owned * owned
    column_sum = lax.psum(jnp.sum(squared, axis=0), ("layer", "row"))
    column_mean = column_sum / total_rows
    return squared / (column_mean[None, :] + 1e-06)


def solution(mesh):
    in_specs = (
        P("row", ("layer", "col")),
        P("row", ("layer", "col")),
        P(("layer", "row"), "col"),
        P(("layer", "row"), "col"),
    )
    out_specs = P(("row", "layer"), "col")
    return jax.shard_map(
        per_device, mesh=mesh, in_specs=in_specs, out_specs=out_specs, check_vma=False
    )
```

profile of v0, /device:TPU:2, one launch (start us, length us, event | category | flops | bytes accessed | tf_op | source)
XLA Modules:
  0.0 1138.5 jit_solution(13868782390979738106)
XLA Ops:
  6.5 0.0 all-gather.2.cloned.1.call-start
  6.5 0.7 convert_element_type.6
  7.2 4.1 copy.6
  11.3 3.0 broadcast_in_dim.4
  14.4 5.7 reshape.10
  20.0 0.0 copy-start.1
  20.1 0.0 copy-start
  20.1 3.5 mul.9
  23.5 0.0 all-gather.2.cloned.1.call-update
  23.6 0.0 reduce-scatter.2.cloned.1.call-start
  23.6 0.0 copy-done.1
  23.6 0.1 broadcast_in_dim.5
  23.8 0.3 reshape.11
  24.1 0.0 copy-done
  24.1 0.1 mul.10
  24.2 10.2 all_gather.7
  34.4 11.2 all-gather.2.cloned.1.call-done
  45.7 15.4 %fusion = f32[8192,1024]{1,0:T(8,128)} fusion(bf16[8192,256]{0,1:T(8,128)(2,1)} %all-gather.2.cloned.1.call-done, bf16[256,1024]{1,0:T(8,128)(2,1)S(1)} %all_gather.7), kind=kOutput, calls=%fused_computation.3 | convolution fusion | flops 4294967296 | bytes 38273024 | tf_op jit(solution)/shard_map/dot_general | solution.py:21
  61.0 0.0 reduce-scatter.2.cloned.1.call-update
  61.1 723.4 %reduce-scatter.2.cloned.1.call-done = f32[128,1024]{1,0:T(8,128)} async-done(((f32[8192,1024]{1,0:T(8,128)}), f32[128,1024]{1,0:T(8,128)}) %reduce-scatter.2.cloned.1.call-update) | async-done | bytes 524304 | tf_op jit(solution)/shard_map/reduce_scatter | solution.py:24
  784.5 1.1 multiply_reduce_fusion
  785.5 344.2 %psum.7 = f32[1024]{0:T(1024)S(1)} all-reduce(f32[1024]{0:T(1024)S(1)} %multiply_reduce_fusion), channel_id=1, replica_groups=mesh['layer'=64,'row'=2,'col'=2] {'layer','row'}, use_global_device_ids=true, to_apply=%region_2.0 | all-reduce | flops 1024 | bytes 8192 | tf_op jit(solution)/shard_map/psum | solution.py:26
  1129.8 1.9 multiply_divide_fusion
  (2 shorter events, 0.0 us)
Async XLA Ops:
  6.5 39.1 %all-gather.2.cloned.1.call-start = ((), (), s32[]{:S(2)}) async-start(), calls=%async_computation.1 | async-start | bytes 6291456 | tf_op jit(solution)/shard_map/all_gather | solution.py:22
  20.0 3.6 copy-start.1
  20.1 4.1 copy-start
  23.6 760.9 %reduce-scatter.2.cloned.1.call-start = ((), (), s32[]{:S(2)}) async-start(), calls=%async_computation.2 | async-start | bytes 34078720 | tf_op jit(solution)/shard_map/reduce_scatter | solution.py:24
Sparse Core Ops, SparseCore 0:
  23.7 21.9 all-gather.1
  61.2 723.2 reduce-scatter.1
where the time goes:
time: 1140 us
  waiting for transfers between devices  735 us (64%)
  blocking collectives  354 us (31%)
  matrix products  15.4 us (1%)
  between operations  13.5 us (1%)
  local copies, waits for them, and re-layouts  13.3 us (1%)
    reduce_scatter x1, waiting for transfers between devices, per_device(): lax.psum_scatter(partial_value, 'layer', scatter_dimension=0, tiled=True)  723 us
    psum x1, blocking collectives, per_device(): column_sum = lax.psum(jnp.sum(squared, axis=0), ('layer', 'row'))  344 us
  transfers between devices with their start and end apart: 2, of which 2 were waited for; matrix products, arithmetic and copies ran while one was open for 0% of the time, Pallas kernels for 0%

commit v1 on v0

v1 whole, which is shorter than its diff:
```python
import functools

import jax
import jax.numpy as jnp
from jax import lax
from jax.experimental import pallas as pl
from jax.experimental.pallas import tpu as pltpu
from jax.sharding import Mesh
from jax.sharding import PartitionSpec as P

NZ, NY, NX = 8, 4, 2
TILE = 64
ALL = ("z", "y", "xl", "xh")
LOW = -2.75
STEP = 13.8 / 65534.0


def lanes(rows):
    return lax.broadcasted_iota(jnp.int32, (rows, 128), 1) < TILE


def mask_kernel(tiles, x_ref, o_ref):
    rows, cols = x_ref.shape
    half = lanes(TILE)
    base = pl.program_id(0) * (rows // TILE)
    for i in range(rows // TILE):
        for g in range(cols // 128):
            keep = jnp.where(half, tiles[base + i, 2 * g], tiles[base + i, 2 * g + 1])
            at = (pl.ds(i * TILE, TILE), pl.ds(g * 128, 128))
            x = x_ref[at].astype(jnp.float32)
            o_ref[at] = jnp.where(keep != 0, x, 0.0).astype(o_ref.dtype)


def masked(x, tiles, block):
    return pl.pallas_call(
        mask_kernel,
        grid=(x.shape[0] // block,),
        in_specs=[
            pl.BlockSpec(memory_space=pltpu.SMEM),
            pl.BlockSpec((block, x.shape[1]), lambda i: (i, 0)),
        ],
        out_specs=pl.BlockSpec((block, x.shape[1]), lambda i: (i, 0)),
        out_shape=jax.ShapeDtypeStruct(x.shape, x.dtype),
        name="mask",
    )(tiles, x)


def encode(p):
    code = jnp.round((jnp.log2(jnp.maximum(p, 0.15)) - LOW) * (1.0 / STEP)) - 32767.0
    return jnp.where(p > 0.0, code, -32768.0).astype(jnp.int32).astype(jnp.int16)


def decode(q):
    f = q.astype(jnp.int32).astype(jnp.float32)
    return jnp.where(f > -32768.0, jnp.exp2((f + 32767.0) * STEP + LOW), 0.0)


def product_kernel(own_ref, other_ref, *refs):
    slabs, (out_ref, left, right, sems) = refs[:-4], refs[-4:]
    z = lax.axis_index("z")
    same = lax.axis_index("xh") == lax.axis_index("core")
    copies = []

    def copy(src, dst):
        copies.append(pltpu.make_async_copy(src, dst, sems.at[len(copies)]))
        copies[-1].start()

    for k in range(NZ):
        copy(own_ref.at[k], left.at[:, pl.ds(256 * k, 128)])
        copy(other_ref.at[k], left.at[:, pl.ds(256 * k + 128, 128)])
    for mine in (True, False):
        slot = jnp.where(same, 0, 1) if mine else jnp.where(same, 1, 0)
        for i, (d, top) in enumerate(OFFSETS):
            ref = slabs[i if mine else i + len(OFFSETS)]
            row = lax.rem(z + d, NZ) * 256 + slot * 128 + top
            copy(ref, right.at[pl.ds(pl.multiple_of(row, 64), ref.shape[0]), :])
    for c in copies:
        c.wait()
    rows = 256
    for m in range(1024 // rows):
        p = jnp.dot(left[pl.ds(m * rows, rows), :], right[...], preferred_element_type=jnp.float32)
        q = encode(p)
        for i in range(rows // 128):
            out_ref[m * rows // 128 + i] = q[i * 128 : (i + 1) * 128]


OFFSETS = ((0, 0), (7, 0), (1, 0), (6, 0), (2, 0), (5, 0), (3, 0), (4, 0), (4, 64))


def product(own, other, slabs):
    n = 16 + len(slabs)
    return pl.pallas_call(
        product_kernel,
        in_specs=[pl.BlockSpec(memory_space=pl.ANY)] * (2 + len(slabs)),
        out_specs=pl.BlockSpec(memory_space=pltpu.VMEM),
        out_shape=jax.ShapeDtypeStruct((8, 128, 1024), jnp.int16),
        scratch_shapes=[
            pltpu.VMEM((1024, 2048), jnp.bfloat16),
            pltpu.VMEM((2048, 1024), jnp.bfloat16),
            pltpu.SemaphoreType.DMA((n,)),
        ],
        compiler_params=pltpu.CompilerParams(vmem_limit_bytes=40 * 2**20),
        cost_estimate=pl.CostEstimate(flops=2 * 1024 * 2048 * 1024, bytes_accessed=10 * 2**20, transcendentals=2**20),
        name="product",
    )(own, other, *slabs)


def square_kernel(q_ref, s_ref, sum_ref):
    total = decode(q_ref[0])
    for i in range(1, 8):
        total = total + decode(q_ref[i])
    s = total * total
    s_ref[...] = s
    sum_ref[...] = jnp.sum(s, axis=0, keepdims=True)


def squares(q):
    return pl.pallas_call(
        square_kernel,
        grid=(4,),
        in_specs=[pl.BlockSpec((8, 128, 256), lambda i: (0, 0, i))],
        out_specs=[pl.BlockSpec((128, 256), lambda i: (0, i)), pl.BlockSpec((1, 256), lambda i: (0, i))],
        out_shape=[jax.ShapeDtypeStruct((128, 1024), jnp.float32), jax.ShapeDtypeStruct((1, 1024), jnp.float32)],
        name="squares",
    )(q)


def gather_slab(block):
    up = functools.partial(lax.ppermute, axis_name="z", perm=[(i, (i + 1) % NZ) for i in range(NZ)])
    down = functools.partial(lax.ppermute, axis_name="z", perm=[(i, (i - 1) % NZ) for i in range(NZ)])
    p1, n1 = up(block), down(block)
    p2, n2 = up(p1), down(n1)
    p3, n3 = up(p2), down(n2)
    p4, n4 = up(p3[:64]), down(n3[64:])
    mine = [block, p1, n1, p2, n2, p3, n3, p4, n4]
    return mine + [lax.ppermute(b, "xh", [(0, 1), (1, 0)]) for b in mine]


def per_device(markov, markov_tiles, slab, slab_tiles):
    right = gather_slab(masked(slab, slab_tiles, 128))
    left = masked(markov, markov_tiles, 1024).reshape(NZ, 1024, 128)
    own = lax.all_to_all(left, "z", 0, 0, tiled=True)
    other = lax.ppermute(own, "core", [(0, 1), (1, 0)])
    codes = product(own, other, right)
    codes = lax.all_to_all(codes, ("y", "xl"), 0, 0, tiled=True)
    squared, sums = squares(codes)
    sums = lax.all_to_all(jnp.broadcast_to(sums[None], (128, 1, 1024)), ALL, 0, 0, tiled=True)
    column_mean = jnp.sum(sums, axis=(0, 1)) / 16384.0
    return squared / (column_mean[None, :] + 1e-06)


def solution(mesh):
    fine = Mesh(mesh.devices.reshape(NZ, NY, NX, 2, 2), ("z", "y", "xl", "xh", "core"))
    layer = ("z", "y", "xl")
    in_specs = (
        P("xh", layer + ("core",)),
        P("xh", layer + ("core",)),
        P(layer + ("xh",), "core"),
        P(layer + ("xh",), "core"),
    )
    return jax.shard_map(
        per_device, mesh=fine, in_specs=in_specs, out_specs=P(("xh",) + layer, "core"), check_vma=False
    )
```

time: 1140 us -> 201 us (0.18)
  waiting for transfers between devices: 735 us -> 34 us
  blocking collectives: 354 us -> 113 us
  starting transfers between devices: 0.04 us -> 27.9 us
  Pallas kernels: 0 us -> 20.1 us
  matrix products: 15.4 us -> 0 us
  between operations: 13.5 us -> 0.06 us
    reduce_scatter x1 -> x0, waiting for transfers between devices: 723 us -> none  [per_device(): lax.psum_scatter(partial_value, 'layer', scatter_dimension=0, tiled=True)]
    psum x1 -> x0, blocking collectives: 344 us -> none  [per_device(): column_sum = lax.psum(jnp.sum(squared, axis=0), ('layer', 'row'))]
    all_to_all x0 -> x3, blocking collectives: none -> 113 us  [the longest x1 59.7 us: per_device(): own = lax.all_to_all(left, 'z', 0, 0, tiled=True)]
    ppermute x0 -> x18, waiting for transfers between devices: none -> 34 us  [the longest x9 20.8 us: gather_slab(): return mine + [lax.ppermute(b, 'xh', [(0, 1), (1, 0)]) for b in mine]]
    ppermute x0 -> x18, starting transfers between devices: none -> 27.9 us  [the longest x9 17.7 us: gather_slab(): return mine + [lax.ppermute(b, 'xh', [(0, 1), (1, 0)]) for b in mine]]
    pallas_call x0 -> x4, Pallas kernels: none -> 20.1 us  [the longest x2 8.46 us: masked(): pl.pallas_call(mask_kernel, grid=(x.shape[0] // block,), in_specs=[pl.Blo...]
    dot_general x1 -> x0, matrix products: 15.4 us -> none  [per_device(): jnp.dot(lax.all_gather(left, 'col', axis=1, tiled=True), inner, preferred...]
  transfers between devices with their start and end apart: 2 -> 18, of which waited for: 2 -> 10; matrix products, arithmetic and copies ran while one was open for 0% -> 0% of each run, Pallas kernels for 0% -> 1%
where the time goes in v1:
time: 201 us; the launch traced here: 200 us
  blocking collectives  113 us (56%)
  waiting for transfers between devices  34 us (17%)
  starting transfers between devices  27.9 us (14%)
  Pallas kernels  20.1 us (10%)
  local copies, waits for them, and re-layouts  3.37 us (2%)
    all_to_all x1, blocking collectives, per_device(): own = lax.all_to_all(left, 'z', 0, 0, tiled=True)  59.7 us
    all_to_all x1, blocking collectives, per_device(): codes = lax.all_to_all(codes, ('y', 'xl'), 0, 0, tiled=True)  29.6 us
    all_to_all x1, blocking collectives, per_device(): lax.all_to_all(jnp.broadcast_to(sums[None], (128, 1, 1024)), ALL, 0, 0, t...  23.7 us
    ppermute x9, waiting for transfers between devices, gather_slab(): return mine + [lax.ppermute(b, 'xh', [(0, 1), (1, 0)]) for b in mine]  20.8 us
    ppermute x9, starting transfers between devices, gather_slab(): return mine + [lax.ppermute(b, 'xh', [(0, 1), (1, 0)]) for b in mine]  17.7 us
    pallas_call x2, Pallas kernels, masked(): pl.pallas_call(mask_kernel, grid=(x.shape[0] // block,), in_specs=[pl.Blo...  8.46 us
    pallas_call x1, Pallas kernels, product(): pl.pallas_call(product_kernel, in_specs=[pl.BlockSpec(memory_space=pl.ANY...  7.6 us
    ppermute x2, waiting for transfers between devices, gather_slab(): p1, n1 = (up(block), down(block))  6.9 us
  transfers between devices with their start and end apart: 18, of which 10 were waited for; matrix products, arithmetic and copies ran while one was open for 0% of the time, Pallas kernels for 1%

profile of v1, /device:TPU:2, one launch (start us, length us, event | category | flops | bytes accessed | tf_op | source)
XLA Modules:
  0.0 199.7 jit_solution(9558921940462941913)
XLA Ops:
  0.0 1.4 copy.7.tiles
  1.4 6.7 %mask.2 = bf16[8192,128]{1,0:T(8,128)(2,1)} custom-call(s32[128,2]{1,0:T(8,128)} %copy.7.tiles, bf16[8192,128]{1,0:T(8,128)(2,1)} %x_ref.2), custom_call_target="tpu_custom_call" | custom-call | tf_op jit(solution)/shard_map/mask/pallas_call | solution.py:35
  8.1 59.7 %all_to_all.15.own_ref = bf16[8,1024,128]{2,1,0:T(8,128)(2,1)S(1)} all-to-all(bf16[8,1024,128]{2,1,0:T(8,128)(2,1)} %bitcast.2), channel_id=1, replica_groups=mesh['z'=8,'y'=4,'xl'=2,'xh'=2,'core'=2] {'z'}, dimensions={0} | all-to-all | bytes 4194304 | tf_op jit(solution)/shard_map/all_to_all | solution.py:142
  67.8 1.7 mask.3.refs_0_
  69.5 2.0 %collective-permute-start.1 = (bf16[128,1024]{1,0:T(8,128)(2,1)}, bf16[128,1024]{1,0:T(8,128)(2,1)S(1)}, u32[]{:S(2)}, u32[]{:S(2)}) collective-permute-start(bf16[128,1024]{1,0:T(8,128)(2,1)} %mask.3.refs_0_), channel_id=1, source_target_pairs={{0,32},{32,64},{64,96},{96,128},{128,160},{160,192},{192,224},{224... | collective-permute-start | bytes 786440 | tf_op jit(solution)/shard_map/ppermute | solution.py:131
  71.6 6.9 %collective-permute-done.2.refs_2_ = bf16[128,1024]{1,0:T(8,128)(2,1)S(1)} collective-permute-done((bf16[128,1024]{1,0:T(8,128)(2,1)}, bf16[128,1024]{1,0:T(8,128)(2,1)S(1)}, u32[]{:S(2)}, u32[]{:S(2)}) %collective-permute-start.2) | collective-permute-done | bytes 262176 | tf_op jit(solution)/shard_map/ppermute | solution.py:131
  78.5 1.5 collective-permute-start.4
  80.5 2.1 %collective-permute-start.9 = (bf16[128,1024]{1,0:T(8,128)(2,1)}, bf16[128,1024]{1,0:T(8,128)(2,1)S(1)}, u32[]{:S(2)}, u32[]{:S(2)}) collective-permute-start(bf16[128,1024]{1,0:T(8,128)(2,1)} %mask.3.refs_0_), channel_id=1, source_target_pairs={{0,2},{2,0},{1,3},{3,1},{4,6},{6,4},{5,7},{7,5},{8,10},{10,8},{9,1... | collective-permute-start | bytes 786440 | tf_op jit(solution)/shard_map/ppermute | solution.py:136
  82.6 3.8 %collective-permute-done.4.refs_4_ = bf16[128,1024]{1,0:T(8,128)(2,1)S(1)} collective-permute-done((bf16[128,1024]{1,0:T(8,128)(2,1)S(1)}, bf16[128,1024]{1,0:T(8,128)(2,1)S(1)}, u32[]{:S(2)}, u32[]{:S(2)}) %collective-permute-start.4) | collective-permute-done | bytes 262176 | tf_op jit(solution)/shard_map/ppermute | solution.py:132
  86.4 2.9 %collective-permute-start.6 = (bf16[128,1024]{1,0:T(8,128)(2,1)S(1)}, bf16[128,1024]{1,0:T(8,128)(2,1)S(1)}, u32[]{:S(2)}, u32[]{:S(2)}) collective-permute-start(bf16[128,1024]{1,0:T(8,128)(2,1)S(1)} %collective-permute-done.4.refs_4_), channel_id=1, source_target_pairs={{0,224},{32,0},{64,32},{96,64},{128,96},{160,128},{192,160},{224,1... | collective-permute-start | bytes 786440 | tf_op jit(solution)/shard_map/ppermute | solution.py:133
  89.3 2.1 %collective-permute-start.11 = (bf16[128,1024]{1,0:T(8,128)(2,1)S(1)}, bf16[128,1024]{1,0:T(8,128)(2,1)S(1)}, u32[]{:S(2)}, u32[]{:S(2)}) collective-permute-start(bf16[128,1024]{1,0:T(8,128)(2,1)S(1)} %collective-permute-done.2.refs_2_), channel_id=1, source_target_pairs={{0,2},{2,0},{1,3},{3,1},{4,6},{6,4},{5,7},{7,5},{8,10},{10,8},{9,1... | collective-permute-start | bytes 786440 | tf_op jit(solution)/shard_map/ppermute | solution.py:136
  91.4 1.4 collective-permute-start.10
  92.9 1.3 collective-permute-done.6.refs_6_
  94.1 2.1 %collective-permute-start.13 = (bf16[128,1024]{1,0:T(8,128)(2,1)S(1)}, bf16[128,1024]{1,0:T(8,128)(2,1)S(1)}, u32[]{:S(2)}, u32[]{:S(2)}) collective-permute-start(bf16[128,1024]{1,0:T(8,128)(2,1)S(1)} %collective-permute-done.4.refs_4_), channel_id=1, source_target_pairs={{0,2},{2,0},{1,3},{3,1},{4,6},{6,4},{5,7},{7,5},{8,10},{10,8},{9,1... | collective-permute-start | bytes 786440 | tf_op jit(solution)/shard_map/ppermute | solution.py:136
  96.2 1.3 collective-permute-done.5.refs_5_
  97.5 2.1 %collective-permute-start.12 = (bf16[128,1024]{1,0:T(8,128)(2,1)S(1)}, bf16[128,1024]{1,0:T(8,128)(2,1)S(1)}, u32[]{:S(2)}, u32[]{:S(2)}) collective-permute-start(bf16[128,1024]{1,0:T(8,128)(2,1)S(1)} %collective-permute-done.3.refs_3_), channel_id=1, source_target_pairs={{0,2},{2,0},{1,3},{3,1},{4,6},{6,4},{5,7},{7,5},{8,10},{10,8},{9,1... | collective-permute-start | bytes 786440 | tf_op jit(solution)/shard_map/ppermute | solution.py:136
  100.1 3.2 %collective-permute-start.8 = (bf16[64,1024]{1,0:T(8,128)(2,1)S(1)}, bf16[64,1024]{1,0:T(8,128)(2,1)S(1)}, u32[]{:S(2)}, u32[]{:S(2)}) collective-permute-start(bf16[64,1024]{1,0:T(8,128)(2,1)S(1)} %slice.9), channel_id=1, source_target_pairs={{0,224},{32,0},{64,32},{96,64},{128,96},{160,128},{192,160},{224,1... | collective-permute-start | bytes 393224 | tf_op jit(solution)/shard_map/ppermute | solution.py:134
  103.3 2.4 %collective-permute-done.10.refs_10_ = bf16[128,1024]{1,0:T(8,128)(2,1)S(1)} collective-permute-done((bf16[128,1024]{1,0:T(8,128)(2,1)S(1)}, bf16[128,1024]{1,0:T(8,128)(2,1)S(1)}, u32[]{:S(2)}, u32[]{:S(2)}) %collective-permute-start.10) | collective-permute-done | bytes 262176 | tf_op jit(solution)/shard_map/ppermute | solution.py:136
  105.7 5.6 %collective-permute-done.13.refs_13_ = bf16[128,1024]{1,0:T(8,128)(2,1)S(1)} collective-permute-done((bf16[128,1024]{1,0:T(8,128)(2,1)S(1)}, bf16[128,1024]{1,0:T(8,128)(2,1)S(1)}, u32[]{:S(2)}, u32[]{:S(2)}) %collective-permute-start.13) | collective-permute-done | bytes 262176 | tf_op jit(solution)/shard_map/ppermute | solution.py:136
  111.3 2.1 %collective-permute-start.15 = (bf16[128,1024]{1,0:T(8,128)(2,1)S(1)}, bf16[128,1024]{1,0:T(8,128)(2,1)S(1)}, u32[]{:S(2)}, u32[]{:S(2)}) collective-permute-start(bf16[128,1024]{1,0:T(8,128)(2,1)S(1)} %collective-permute-done.6.refs_6_), channel_id=1, source_target_pairs={{0,2},{2,0},{1,3},{3,1},{4,6},{6,4},{5,7},{7,5},{8,10},{10,8},{9,1... | collective-permute-start | bytes 786440 | tf_op jit(solution)/shard_map/ppermute | solution.py:136
  113.4 3.5 %collective-permute-done.12.refs_12_ = bf16[128,1024]{1,0:T(8,128)(2,1)S(1)} collective-permute-done((bf16[128,1024]{1,0:T(8,128)(2,1)S(1)}, bf16[128,1024]{1,0:T(8,128)(2,1)S(1)}, u32[]{:S(2)}, u32[]{:S(2)}) %collective-permute-start.12) | collective-permute-done | bytes 262176 | tf_op jit(solution)/shard_map/ppermute | solution.py:136
  116.9 2.1 %collective-permute-start.14 = (bf16[128,1024]{1,0:T(8,128)(2,1)S(1)}, bf16[128,1024]{1,0:T(8,128)(2,1)S(1)}, u32[]{:S(2)}, u32[]{:S(2)}) collective-permute-start(bf16[128,1024]{1,0:T(8,128)(2,1)S(1)} %collective-permute-done.5.refs_5_), channel_id=1, source_target_pairs={{0,2},{2,0},{1,3},{3,1},{4,6},{6,4},{5,7},{7,5},{8,10},{10,8},{9,1... | collective-permute-start | bytes 786440 | tf_op jit(solution)/shard_map/ppermute | solution.py:136
  119.0 1.4 collective-permute-start.17
  120.5 2.1 %collective-permute-start.16 = (bf16[64,1024]{1,0:T(8,128)(2,1)S(1)}, bf16[64,1024]{1,0:T(8,128)(2,1)S(1)}, u32[]{:S(2)}, u32[]{:S(2)}) collective-permute-start(bf16[64,1024]{1,0:T(8,128)(2,1)S(1)} %collective-permute-done.7.refs_7_), channel_id=1, source_target_pairs={{0,2},{2,0},{1,3},{3,1},{4,6},{6,4},{5,7},{7,5},{8,10},{10,8},{9,1... | collective-permute-start | bytes 393224 | tf_op jit(solution)/shard_map/ppermute | solution.py:136
  122.6 7.5 %collective-permute-done.17.refs_17_ = bf16[64,1024]{1,0:T(8,128)(2,1)S(1)} collective-permute-done((bf16[64,1024]{1,0:T(8,128)(2,1)S(1)}, bf16[64,1024]{1,0:T(8,128)(2,1)S(1)}, u32[]{:S(2)}, u32[]{:S(2)}) %collective-permute-start.17) | collective-permute-done | bytes 131104 | tf_op jit(solution)/shard_map/ppermute | solution.py:136
  130.1 1.4 collective-permute-done.16.refs_16_
  131.6 0.9 copy-done
  132.5 7.6 %product.1 = s16[8,128,1024]{2,1,0:T(8,128)(2,1)S(1)} custom-call(bf16[8,1024,128]{2,1,0:T(8,128)(2,1)S(1)} %all_to_all.15.own_ref, bf16[8,1024,128]{2,1,0:T(8,128)(2,1)} %collective-permute-done.other_ref, bf16[128,1024]{1,0:T(8,128)(2,1)S(1)} %copy-done, bf16[128,1024]{1,0:T(8,128)(2,1)S(1)} %collective-permute-done.1.refs_1_, ...), custom_call_target="tpu_custom_call" | custom-call | flops 4294967296 | bytes 10485760 | tf_op jit(solution)/shard_map/product/pallas_call | solution.py:92
  140.1 29.6 %all_to_all.16.q_ref = s16[8,128,1024]{2,1,0:T(8,128)(2,1)} all-to-all(s16[8,128,1024]{2,1,0:T(8,128)(2,1)S(1)} %product.1), channel_id=1, replica_groups=mesh['z'=8,'y'=4,'xl'=2,'xh'=2,'core'=2] {'y','xl'}, dimensions={0} | all-to-all | bytes 4194304 | tf_op jit(solution)/shard_map/all_to_all | solution.py:145
  169.7 4.1 %squares.1 = (f32[128,1024]{1,0:T(8,128)}, f32[1,1024]{1,0:T(1,128)}) custom-call(s16[8,128,1024]{2,1,0:T(8,128)(2,1)} %all_to_all.16.q_ref), custom_call_target="tpu_custom_call" | custom-call | tf_op jit(solution)/shard_map/squares/pallas_call | solution.py:118
  173.8 1.0 broadcast_in_dim.10
  174.8 23.7 %all_to_all.17 = f32[128,1,1024]{2,1,0:T(1,128)S(1)} all-to-all(f32[128,1,1024]{2,1,0:T(1,128)S(1)} %broadcast_in_dim.10), channel_id=1, replica_groups=mesh['z'=8,'y'=4,'xl'=2,'xh'=2,'core'=2] {'z','y','xl','xh'}, dimensions={0} | all-to-all | bytes 1048576 | tf_op jit(solution)/shard_map/all_to_all | solution.py:147
  (22 shorter events, 2.2 us)
Async XLA Ops:
  67.8 63.7 %collective-permute-start = (bf16[8,1024,128]{2,1,0:T(8,128)(2,1)S(1)}, bf16[8,1024,128]{2,1,0:T(8,128)(2,1)}, u32[]{:S(2)}, u32[]{:S(2)}) collective-permute-start(bf16[8,1024,128]{2,1,0:T(8,128)(2,1)S(1)} %all_to_all.15.own_ref), channel_id=1, source_target_pairs={{0,1},{1,0},{2,3},{3,2},{4,5},{5,4},{6,7},{7,6},{8,9},{9,8},{10,11... | collective-permute-start | bytes 6291464 | tf_op jit(solution)/shard_map/ppermute | solution.py:143
  69.5 8.9 %collective-permute-start.2 = (bf16[128,1024]{1,0:T(8,128)(2,1)}, bf16[128,1024]{1,0:T(8,128)(2,1)S(1)}, u32[]{:S(2)}, u32[]{:S(2)}) collective-permute-start(bf16[128,1024]{1,0:T(8,128)(2,1)} %mask.3.refs_0_), channel_id=1, source_target_pairs={{0,224},{32,0},{64,32},{96,64},{128,96},{160,128},{192,160},{224,1... | collective-permute-start | bytes 786440 | tf_op jit(solution)/shard_map/ppermute | solution.py:131
  69.5 10.4 %collective-permute-start.1 = (bf16[128,1024]{1,0:T(8,128)(2,1)}, bf16[128,1024]{1,0:T(8,128)(2,1)S(1)}, u32[]{:S(2)}, u32[]{:S(2)}) collective-permute-start(bf16[128,1024]{1,0:T(8,128)(2,1)} %mask.3.refs_0_), channel_id=1, source_target_pairs={{0,32},{32,64},{64,96},{96,128},{128,160},{160,192},{192,224},{224... | collective-permute-start | bytes 786440 | tf_op jit(solution)/shard_map/ppermute | solution.py:131
  78.5 7.9 %collective-permute-start.4 = (bf16[128,1024]{1,0:T(8,128)(2,1)S(1)}, bf16[128,1024]{1,0:T(8,128)(2,1)S(1)}, u32[]{:S(2)}, u32[]{:S(2)}) collective-permute-start(bf16[128,1024]{1,0:T(8,128)(2,1)S(1)} %collective-permute-done.2.refs_2_), channel_id=1, source_target_pairs={{0,224},{32,0},{64,32},{96,64},{128,96},{160,128},{192,160},{224,1... | collective-permute-start | bytes 786440 | tf_op jit(solution)/shard_map/ppermute | solution.py:132
  80.0 9.4 %collective-permute-start.3 = (bf16[128,1024]{1,0:T(8,128)(2,1)S(1)}, bf16[128,1024]{1,0:T(8,128)(2,1)S(1)}, u32[]{:S(2)}, u32[]{:S(2)}) collective-permute-start(bf16[128,1024]{1,0:T(8,128)(2,1)S(1)} %collective-permute-done.1.refs_1_), channel_id=1, source_target_pairs={{0,32},{32,64},{64,96},{96,128},{128,160},{160,192},{192,224},{224... | collective-permute-start | bytes 786440 | tf_op jit(solution)/shard_map/ppermute | solution.py:132
  80.5 10.9 %collective-permute-start.9 = (bf16[128,1024]{1,0:T(8,128)(2,1)}, bf16[128,1024]{1,0:T(8,128)(2,1)S(1)}, u32[]{:S(2)}, u32[]{:S(2)}) collective-permute-start(bf16[128,1024]{1,0:T(8,128)(2,1)} %mask.3.refs_0_), channel_id=1, source_target_pairs={{0,2},{2,0},{1,3},{3,1},{4,6},{6,4},{5,7},{7,5},{8,10},{10,8},{9,1... | collective-permute-start | bytes 786440 | tf_op jit(solution)/shard_map/ppermute | solution.py:136
  86.4 7.7 %collective-permute-start.6 = (bf16[128,1024]{1,0:T(8,128)(2,1)S(1)}, bf16[128,1024]{1,0:T(8,128)(2,1)S(1)}, u32[]{:S(2)}, u32[]{:S(2)}) collective-permute-start(bf16[128,1024]{1,0:T(8,128)(2,1)S(1)} %collective-permute-done.4.refs_4_), channel_id=1, source_target_pairs={{0,224},{32,0},{64,32},{96,64},{128,96},{160,128},{192,160},{224,1... | collective-permute-start | bytes 786440 | tf_op jit(solution)/shard_map/ppermute | solution.py:133
  89.3 8.2 %collective-permute-start.5 = (bf16[128,1024]{1,0:T(8,128)(2,1)S(1)}, bf16[128,1024]{1,0:T(8,128)(2,1)S(1)}, u32[]{:S(2)}, u32[]{:S(2)}) collective-permute-start(bf16[128,1024]{1,0:T(8,128)(2,1)S(1)} %collective-permute-done.3.refs_3_), channel_id=1, source_target_pairs={{0,32},{32,64},{64,96},{96,128},{128,160},{160,192},{192,224},{224... | collective-permute-start | bytes 786440 | tf_op jit(solution)/shard_map/ppermute | solution.py:133
  89.3 10.7 %collective-permute-start.11 = (bf16[128,1024]{1,0:T(8,128)(2,1)S(1)}, bf16[128,1024]{1,0:T(8,128)(2,1)S(1)}, u32[]{:S(2)}, u32[]{:S(2)}) collective-permute-start(bf16[128,1024]{1,0:T(8,128)(2,1)S(1)} %collective-permute-done.2.refs_2_), channel_id=1, source_target_pairs={{0,2},{2,0},{1,3},{3,1},{4,6},{6,4},{5,7},{7,5},{8,10},{10,8},{9,1... | collective-permute-start | bytes 786440 | tf_op jit(solution)/shard_map/ppermute | solution.py:136
  91.4 14.2 %collective-permute-start.10 = (bf16[128,1024]{1,0:T(8,128)(2,1)S(1)}, bf16[128,1024]{1,0:T(8,128)(2,1)S(1)}, u32[]{:S(2)}, u32[]{:S(2)}) collective-permute-start(bf16[128,1024]{1,0:T(8,128)(2,1)S(1)} %collective-permute-done.1.refs_1_), channel_id=1, source_target_pairs={{0,2},{2,0},{1,3},{3,1},{4,6},{6,4},{5,7},{7,5},{8,10},{10,8},{9,1... | collective-permute-start | bytes 786440 | tf_op jit(solution)/shard_map/ppermute | solution.py:136
  94.1 17.2 %collective-permute-start.13 = (bf16[128,1024]{1,0:T(8,128)(2,1)S(1)}, bf16[128,1024]{1,0:T(8,128)(2,1)S(1)}, u32[]{:S(2)}, u32[]{:S(2)}) collective-permute-start(bf16[128,1024]{1,0:T(8,128)(2,1)S(1)} %collective-permute-done.4.refs_4_), channel_id=1, source_target_pairs={{0,2},{2,0},{1,3},{3,1},{4,6},{6,4},{5,7},{7,5},{8,10},{10,8},{9,1... | collective-permute-start | bytes 786440 | tf_op jit(solution)/shard_map/ppermute | solution.py:136
  97.5 19.4 %collective-permute-start.12 = (bf16[128,1024]{1,0:T(8,128)(2,1)S(1)}, bf16[128,1024]{1,0:T(8,128)(2,1)S(1)}, u32[]{:S(2)}, u32[]{:S(2)}) collective-permute-start(bf16[128,1024]{1,0:T(8,128)(2,1)S(1)} %collective-permute-done.3.refs_3_), channel_id=1, source_target_pairs={{0,2},{2,0},{1,3},{3,1},{4,6},{6,4},{5,7},{7,5},{8,10},{10,8},{9,1... | collective-permute-start | bytes 786440 | tf_op jit(solution)/shard_map/ppermute | solution.py:136
  100.1 19.0 %collective-permute-start.8 = (bf16[64,1024]{1,0:T(8,128)(2,1)S(1)}, bf16[64,1024]{1,0:T(8,128)(2,1)S(1)}, u32[]{:S(2)}, u32[]{:S(2)}) collective-permute-start(bf16[64,1024]{1,0:T(8,128)(2,1)S(1)} %slice.9), channel_id=1, source_target_pairs={{0,224},{32,0},{64,32},{96,64},{128,96},{160,128},{192,160},{224,1... | collective-permute-start | bytes 393224 | tf_op jit(solution)/shard_map/ppermute | solution.py:134
  105.7 14.8 %collective-permute-start.7 = (bf16[64,1024]{1,0:T(8,128)(2,1)S(1)}, bf16[64,1024]{1,0:T(8,128)(2,1)S(1)}, u32[]{:S(2)}, u32[]{:S(2)}) collective-permute-start(bf16[64,1024]{1,0:T(8,128)(2,1)S(1)} %slice.8), channel_id=1, source_target_pairs={{0,32},{32,64},{64,96},{96,128},{128,160},{160,192},{192,224},{224... | collective-permute-start | bytes 393224 | tf_op jit(solution)/shard_map/ppermute | solution.py:134
  111.3 20.2 %collective-permute-start.15 = (bf16[128,1024]{1,0:T(8,128)(2,1)S(1)}, bf16[128,1024]{1,0:T(8,128)(2,1)S(1)}, u32[]{:S(2)}, u32[]{:S(2)}) collective-permute-start(bf16[128,1024]{1,0:T(8,128)(2,1)S(1)} %collective-permute-done.6.refs_6_), channel_id=1, source_target_pairs={{0,2},{2,0},{1,3},{3,1},{4,6},{6,4},{5,7},{7,5},{8,10},{10,8},{9,1... | collective-permute-start | bytes 786440 | tf_op jit(solution)/shard_map/ppermute | solution.py:136
  116.9 14.6 %collective-permute-start.14 = (bf16[128,1024]{1,0:T(8,128)(2,1)S(1)}, bf16[128,1024]{1,0:T(8,128)(2,1)S(1)}, u32[]{:S(2)}, u32[]{:S(2)}) collective-permute-start(bf16[128,1024]{1,0:T(8,128)(2,1)S(1)} %collective-permute-done.5.refs_5_), channel_id=1, source_target_pairs={{0,2},{2,0},{1,3},{3,1},{4,6},{6,4},{5,7},{7,5},{8,10},{10,8},{9,1... | collective-permute-start | bytes 786440 | tf_op jit(solution)/shard_map/ppermute | solution.py:136
  119.0 11.1 %collective-permute-start.17 = (bf16[64,1024]{1,0:T(8,128)(2,1)S(1)}, bf16[64,1024]{1,0:T(8,128)(2,1)S(1)}, u32[]{:S(2)}, u32[]{:S(2)}) collective-permute-start(bf16[64,1024]{1,0:T(8,128)(2,1)S(1)} %collective-permute-done.8.refs_8_), channel_id=1, source_target_pairs={{0,2},{2,0},{1,3},{3,1},{4,6},{6,4},{5,7},{7,5},{8,10},{10,8},{9,1... | collective-permute-start | bytes 393224 | tf_op jit(solution)/shard_map/ppermute | solution.py:136
  120.5 11.1 %collective-permute-start.16 = (bf16[64,1024]{1,0:T(8,128)(2,1)S(1)}, bf16[64,1024]{1,0:T(8,128)(2,1)S(1)}, u32[]{:S(2)}, u32[]{:S(2)}) collective-permute-start(bf16[64,1024]{1,0:T(8,128)(2,1)S(1)} %collective-permute-done.7.refs_7_), channel_id=1, source_target_pairs={{0,2},{2,0},{1,3},{3,1},{4,6},{6,4},{5,7},{7,5},{8,10},{10,8},{9,1... | collective-permute-start | bytes 393224 | tf_op jit(solution)/shard_map/ppermute | solution.py:136
  131.5 1.0 copy-start
  173.8 25.0 %copy-start.1 = (f32[128,1024]{1,0:T(8,128)S(1)}, f32[128,1024]{1,0:T(8,128)}, u32[]{:S(2)}) copy-start(f32[128,1024]{1,0:T(8,128)} %get-tuple-element.7) | copy-start | bytes 1572868

commit v2 on v1

--- a/solution.py
+++ b/solution.py
@@ -10,6 +10,7 @@
 
 NZ, NY, NX = 8, 4, 2
 TILE = 64
+CAP = 12
 ALL = ("z", "y", "xl", "xh")
 LOW = -2.75
 STEP = 13.8 / 65534.0
@@ -43,6 +44,76 @@
         out_shape=jax.ShapeDtypeStruct(x.shape, x.dtype),
         name="mask",
     )(tiles, x)
+
+
+def halves(x):
+    return jnp.concatenate([x[:, TILE:], x[:, :TILE]], axis=1)
+
+
+def pack_kernel(tiles, flags_ref, x_ref, o_ref):
+    left = (lax.broadcasted_iota(jnp.int32, (32, 128), 1) < TILE).astype(jnp.float32).astype(x_ref.dtype)
+    right = 1 - left
+    base = pl.program_id(0) * 16
+    o_ref[...] = jnp.zeros_like(o_ref)
+    slot = 0
+    for i in range(16):
+        top, bottom = x_ref[pl.ds(i * TILE, 32), :], x_ref[pl.ds(i * TILE + 32, 32), :]
+        pair = (top * left + halves(bottom) * right, halves(top) * left + bottom * right)
+        for j in range(2):
+            o_ref[0, pl.ds(pl.multiple_of(slot * 32, 32), 32), :] = pair[j]
+            slot = jnp.minimum(slot + tiles[base + i, j], CAP)
+    o_ref[0, pl.ds(CAP * 32, 32), :] = jnp.zeros((32, 128), o_ref.dtype)
+    o_ref[0, pl.ds(CAP * 32 + 32, 16), :] = flags_ref[...]
+
+
+def pack(markov, tiles):
+    flags = jnp.pad(tiles.astype(markov.dtype), ((0, 0), (0, 126)))
+    return pl.pallas_call(
+        pack_kernel,
+        grid=(NZ,),
+        in_specs=[
+            pl.BlockSpec(memory_space=pltpu.SMEM),
+            pl.BlockSpec((16, 128), lambda i: (i, 0)),
+            pl.BlockSpec((1024, 128), lambda i: (i, 0)),
+        ],
+        out_specs=pl.BlockSpec((1, CAP * 32 + 48, 128), lambda i: (i, 0, 0)),
+        out_shape=jax.ShapeDtypeStruct((NZ, CAP * 32 + 48, 128), markov.dtype),
+        name="pack",
+    )(tiles, flags, markov)
+
+
+def unpack_kernel(flags, x_ref, o_ref):
+    left = (lax.broadcasted_iota(jnp.int32, (32, 128), 1) < TILE).astype(jnp.float32).astype(x_ref.dtype)
+    right = 1 - left
+    base = pl.program_id(0) * 32
+    slot = 0
+    for i in range(16):
+        pair = []
+        for j in range(2):
+            flag = flags[base + 2 * i + j]
+            at = jnp.minimum(jnp.where(flag > 0, slot, CAP), CAP)
+            pair.append(x_ref[0, pl.ds(pl.multiple_of(at * 32, 32), 32), :])
+            slot = slot + flag
+        o_ref[0, pl.ds(i * TILE, 32), :] = pair[0] * left + halves(pair[1]) * right
+        o_ref[0, pl.ds(i * TILE + 32, 32), :] = halves(pair[0]) * left + pair[1] * right
+
+
+def unpack(packed, flags):
+    return pl.pallas_call(
+        unpack_kernel,
+        grid=(NZ,),
+        in_specs=[
+            pl.BlockSpec(memory_space=pltpu.SMEM),
+            pl.BlockSpec((1, CAP * 32 + 48, 128), lambda i: (i, 0, 0)),
+        ],
+        out_specs=pl.BlockSpec((1, 1024, 128), lambda i: (i, 0, 0)),
+        out_shape=jax.ShapeDtypeStruct((NZ, 1024, 128), packed.dtype),
+        name="unpack",
+    )(flags, packed)
+
+
+def flags_of(packed):
+    return packed[:, CAP * 32 + 32 :, :2].astype(jnp.int32).reshape(NZ, 32)
 
 
 def encode(p):
@@ -105,24 +176,27 @@
     )(own, other, *slabs)
 
 
-def square_kernel(q_ref, s_ref, sum_ref):
+def square_kernel(bad, q_ref, s_ref, sum_ref):
     total = decode(q_ref[0])
     for i in range(1, 8):
         total = total + decode(q_ref[i])
     s = total * total
     s_ref[...] = s
-    sum_ref[...] = jnp.sum(s, axis=0, keepdims=True)
-
-
-def squares(q):
+    sum_ref[...] = jnp.sum(s, axis=0, keepdims=True) + bad[0]
+
+
+def squares(q, bad):
     return pl.pallas_call(
         square_kernel,
         grid=(4,),
-        in_specs=[pl.BlockSpec((8, 128, 256), lambda i: (0, 0, i))],
+        in_specs=[
+            pl.BlockSpec(memory_space=pltpu.SMEM),
+            pl.BlockSpec((8, 128, 256), lambda i: (0, 0, i)),
+        ],
         out_specs=[pl.BlockSpec((128, 256), lambda i: (0, i)), pl.BlockSpec((1, 256), lambda i: (0, i))],
         out_shape=[jax.ShapeDtypeStruct((128, 1024), jnp.float32), jax.ShapeDtypeStruct((1, 1024), jnp.float32)],
         name="squares",
-    )(q)
+    )(bad, q)
 
 
 def gather_slab(block):
@@ -136,17 +210,46 @@
     return mine + [lax.ppermute(b, "xh", [(0, 1), (1, 0)]) for b in mine]
 
 
-def per_device(markov, markov_tiles, slab, slab_tiles):
+def finish(own, other, right, bad):
+    codes = product(own, other, right)
+    codes = lax.all_to_all(codes, ("y", "xl"), 0, 0, tiled=True)
+    squared, sums = squares(codes, bad)
+    for axes, n in ((("y", "xl", "xh"), 16), ("z", 8)):
+        sums = lax.all_to_all(jnp.broadcast_to(sums[None], (n, 1, 1024)), axes, 0, 0, tiled=True)
+        sums = jnp.sum(sums, axis=0)
+    return squared, sums
+
+
+def inflate(squared, sums):
+    return squared / (sums / 16384.0 + 1e-06)
+
+
+def swap_core(x):
+    return lax.ppermute(x, "core", [(0, 1), (1, 0)])
+
+
+def dense(markov, markov_tiles, slab, slab_tiles):
     right = gather_slab(masked(slab, slab_tiles, 128))
     left = masked(markov, markov_tiles, 1024).reshape(NZ, 1024, 128)
     own = lax.all_to_all(left, "z", 0, 0, tiled=True)
-    other = lax.ppermute(own, "core", [(0, 1), (1, 0)])
-    codes = product(own, other, right)
-    codes = lax.all_to_all(codes, ("y", "xl"), 0, 0, tiled=True)
-    squared, sums = squares(codes)
-    sums = lax.all_to_all(jnp.broadcast_to(sums[None], (128, 1, 1024)), ALL, 0, 0, tiled=True)
-    column_mean = jnp.sum(sums, axis=(0, 1)) / 16384.0
-    return squared / (column_mean[None, :] + 1e-06)
+    return inflate(*finish(own, swap_core(own), right, jnp.zeros((1,), jnp.float32)))
+
+
+def per_device(markov, markov_tiles, slab, slab_tiles):
+    right = gather_slab(masked(slab, slab_tiles, 128))
+    own = lax.all_to_all(pack(markov, markov_tiles), "z", 0, 0, tiled=True)
+    other = swap_core(own)
+    own_flags, other_flags = flags_of(own), flags_of(other)
+    counts = jnp.maximum(jnp.max(jnp.sum(own_flags, axis=1)), jnp.max(jnp.sum(other_flags, axis=1)))
+    bad = jnp.where(counts > CAP, jnp.inf, 0.0).astype(jnp.float32).reshape(1)
+    squared, sums = finish(
+        unpack(own, own_flags.reshape(-1)), unpack(other, other_flags.reshape(-1)), right, bad
+    )
+    return lax.cond(
+        sums[0, 0] > 1e30,
+        lambda: dense(markov, markov_tiles, slab, slab_tiles),
+        lambda: inflate(squared, sums),
+    )
 
 
 def solution(mesh):

time: 201 us -> 184 us (0.915)
  blocking collectives: 113 us -> 12.3 us
  waiting for transfers between devices: 34 us -> 63.4 us
  starting transfers between devices: 27.9 us -> 47.6 us
  local copies, waits for them, and re-layouts: 3.37 us -> 17.6 us
  Pallas kernels: 20.1 us -> 32.8 us
  other arithmetic: 1.21 us -> 6.5 us
  between operations: 0.06 us -> 2.18 us
    all_to_all x3 -> x1, blocking collectives: 113 us -> 12.3 us  [finish(): lax.all_to_all(jnp.broadcast_to(sums[None], (n, 1, 1024)), axes, 0, 0, ti...]
    all_to_all x0 -> x3, waiting for transfers between devices: none -> 25.5 us  [the longest x1 17.4 us: finish(): codes = lax.all_to_all(codes, ('y', 'xl'), 0, 0, tiled=True)]
    all_to_all x0 -> x3, starting transfers between devices: none -> 21.3 us  [the longest x1 8.47 us: per_device(): own = lax.all_to_all(pack(markov, markov_tiles), 'z', 0, 0, tiled=True)]
    pallas_call x1 -> x4, Pallas kernels: 4.07 us -> 22.8 us  [the longest x2 12.1 us: unpack(): pl.pallas_call(unpack_kernel, grid=(NZ,), in_specs=[pl.BlockSpec(memory_s...]
    ppermute x2, waiting for transfers between devices: 6.9 us -> 22.4 us  [gather_slab(): p1, n1 = (up(block), down(block))]
    ppermute x9, waiting for transfers between devices: 20.8 us -> 7.62 us  [gather_slab(): return mine + [lax.ppermute(b, 'xh', [(0, 1), (1, 0)]) for b in mine]]
    unnamed x5 -> x41, local copies, waits for them, and re-layouts: 2.36 us -> 12.1 us
    pallas_call x2 -> x1, Pallas kernels: 8.46 us -> 1.31 us  [masked(): pl.pallas_call(mask_kernel, grid=(x.shape[0] // block,), in_specs=[pl.Blo...]
  transfers between devices with their start and end apart: 18 -> 21, of which waited for: 10 -> 9; matrix products, arithmetic and copies ran while one was open for 0% -> 5% of each run, Pallas kernels for 1% -> 7%
where the time goes in v2:
time: 184 us; the launch traced here: 183 us
  waiting for transfers between devices  63.4 us (34%)
  starting transfers between devices  47.6 us (26%)
  Pallas kernels  32.8 us (18%)
  local copies, waits for them, and re-layouts  17.6 us (10%)
  blocking collectives  12.3 us (7%)
  other arithmetic  6.5 us (4%)
  between operations  2.18 us (1%)
    ppermute x2, waiting for transfers between devices, gather_slab(): p1, n1 = (up(block), down(block))  22.4 us
    all_to_all x1, waiting for transfers between devices, finish(): codes = lax.all_to_all(codes, ('y', 'xl'), 0, 0, tiled=True)  17.4 us
    ppermute x9, starting transfers between devices, gather_slab(): return mine + [lax.ppermute(b, 'xh', [(0, 1), (1, 0)]) for b in mine]  17.1 us
    all_to_all x1, blocking collectives, finish(): lax.all_to_all(jnp.broadcast_to(sums[None], (n, 1, 1024)), axes, 0, 0, ti...  12.3 us
    pallas_call x2, Pallas kernels, unpack(): pl.pallas_call(unpack_kernel, grid=(NZ,), in_specs=[pl.BlockSpec(memory_s...  12.1 us
    unnamed x41, local copies, waits for them, and re-layouts  12.1 us
    pallas_call x1, Pallas kernels, product(): pl.pallas_call(product_kernel, in_specs=[pl.BlockSpec(memory_space=pl.ANY...  8.66 us
    all_to_all x1, starting transfers between devices, per_device(): own = lax.all_to_all(pack(markov, markov_tiles), 'z', 0, 0, tiled=True)  8.47 us
  transfers between devices with their start and end apart: 21, of which 9 were waited for; matrix products, arithmetic and copies ran while one was open for 5% of the time, Pallas kernels for 7%

profile of v2, /device:TPU:2, one launch (start us, length us, event | category | flops | bytes accessed | tf_op | source)
XLA Modules:
  0.0 182.6 jit_solution(3290902428185706196)
XLA Ops:
  0.7 1.4 copy.26.tiles
  2.9 6.8 %pack.1 = bf16[8,432,128]{2,1,0:T(8,128)(2,1)} custom-call(s32[128,2]{1,0:T(8,128)} %copy.26.tiles, bf16[128,128]{1,0:T(8,128)(2,1)} %pad.4.flags_ref, bf16[8192,128]{1,0:T(8,128)(2,1)} %x_ref.2), custom_call_target="tpu_custom_call" | custom-call | tf_op jit(solution)/shard_map/pack/pallas_call | solution.py:71
  9.7 8.5 %all-to-all-start.4 = ((bf16[8,432,128]{2,1,0:T(8,128)(2,1)}), bf16[8,432,128]{2,1,0:T(8,128)(2,1)}, u32[]{:S(2)}, u32[]{:S(2)}) async-start(bf16[8,432,128]{2,1,0:T(8,128)(2,1)} %pack.1), calls=%async_computation.4 | async-start | bytes 1769472 | tf_op jit(solution)/shard_map/all_to_all | solution.py:240
  19.5 3.2 %collective-permute-start.20 = (bf16[128,1024]{1,0:T(8,128)(2,1)}, bf16[128,1024]{1,0:T(8,128)(2,1)S(1)}, u32[]{:S(2)}, u32[]{:S(2)}) collective-permute-start(bf16[128,1024]{1,0:T(8,128)(2,1)} %mask.5.refs_0_), channel_id=1, source_target_pairs={{0,224},{32,0},{64,32},{96,64},{128,96},{160,128},{192,160},{224,1... | collective-permute-start | bytes 786440 | tf_op jit(solution)/shard_map/ppermute | solution.py:205
  22.7 22.4 %collective-permute-done.20.refs_2_ = bf16[128,1024]{1,0:T(8,128)(2,1)S(1)} collective-permute-done((bf16[128,1024]{1,0:T(8,128)(2,1)}, bf16[128,1024]{1,0:T(8,128)(2,1)S(1)}, u32[]{:S(2)}, u32[]{:S(2)}) %collective-permute-start.20) | collective-permute-done | bytes 262176 | tf_op jit(solution)/shard_map/ppermute | solution.py:205
  45.1 1.5 collective-permute-start.22
  47.2 2.1 %collective-permute-start.27 = (bf16[128,1024]{1,0:T(8,128)(2,1)}, bf16[128,1024]{1,0:T(8,128)(2,1)S(1)}, u32[]{:S(2)}, u32[]{:S(2)}) collective-permute-start(bf16[128,1024]{1,0:T(8,128)(2,1)} %mask.5.refs_0_), channel_id=1, source_target_pairs={{0,2},{2,0},{1,3},{3,1},{4,6},{6,4},{5,7},{7,5},{8,10},{10,8},{9,1... | collective-permute-start | bytes 786440 | tf_op jit(solution)/shard_map/ppermute | solution.py:210
  49.3 2.6 %collective-permute-done.22.refs_4_ = bf16[128,1024]{1,0:T(8,128)(2,1)S(1)} collective-permute-done((bf16[128,1024]{1,0:T(8,128)(2,1)S(1)}, bf16[128,1024]{1,0:T(8,128)(2,1)S(1)}, u32[]{:S(2)}, u32[]{:S(2)}) %collective-permute-start.22) | collective-permute-done | bytes 262176 | tf_op jit(solution)/shard_map/ppermute | solution.py:206
  51.9 3.0 %collective-permute-start.24 = (bf16[128,1024]{1,0:T(8,128)(2,1)S(1)}, bf16[128,1024]{1,0:T(8,128)(2,1)S(1)}, u32[]{:S(2)}, u32[]{:S(2)}) collective-permute-start(bf16[128,1024]{1,0:T(8,128)(2,1)S(1)} %collective-permute-done.22.refs_4_), channel_id=1, source_target_pairs={{0,224},{32,0},{64,32},{96,64},{128,96},{160,128},{192,160},{224,1... | collective-permute-start | bytes 786440 | tf_op jit(solution)/shard_map/ppermute | solution.py:207
  54.9 1.7 collective-permute-done.21.refs_3_
  56.6 2.1 %collective-permute-start.29 = (bf16[128,1024]{1,0:T(8,128)(2,1)S(1)}, bf16[128,1024]{1,0:T(8,128)(2,1)S(1)}, u32[]{:S(2)}, u32[]{:S(2)}) collective-permute-start(bf16[128,1024]{1,0:T(8,128)(2,1)S(1)} %collective-permute-done.20.refs_2_), channel_id=1, source_target_pairs={{0,2},{2,0},{1,3},{3,1},{4,6},{6,4},{5,7},{7,5},{8,10},{10,8},{9,1... | collective-permute-start | bytes 786440 | tf_op jit(solution)/shard_map/ppermute | solution.py:210
  58.7 1.4 collective-permute-start.28
  60.1 2.1 %collective-permute-start.31 = (bf16[128,1024]{1,0:T(8,128)(2,1)S(1)}, bf16[128,1024]{1,0:T(8,128)(2,1)S(1)}, u32[]{:S(2)}, u32[]{:S(2)}) collective-permute-start(bf16[128,1024]{1,0:T(8,128)(2,1)S(1)} %collective-permute-done.22.refs_4_), channel_id=1, source_target_pairs={{0,2},{2,0},{1,3},{3,1},{4,6},{6,4},{5,7},{7,5},{8,10},{10,8},{9,1... | collective-permute-start | bytes 786440 | tf_op jit(solution)/shard_map/ppermute | solution.py:210
  62.3 3.6 %collective-permute-done.23.refs_5_ = bf16[128,1024]{1,0:T(8,128)(2,1)S(1)} collective-permute-done((bf16[128,1024]{1,0:T(8,128)(2,1)}, bf16[128,1024]{1,0:T(8,128)(2,1)S(1)}, u32[]{:S(2)}, u32[]{:S(2)}) %collective-permute-start.23) | collective-permute-done | bytes 262176 | tf_op jit(solution)/shard_map/ppermute | solution.py:207
  68.1 2.1 %collective-permute-start.30 = (bf16[128,1024]{1,0:T(8,128)(2,1)}, bf16[128,1024]{1,0:T(8,128)(2,1)}, u32[]{:S(2)}, u32[]{:S(2)}) collective-permute-start(bf16[128,1024]{1,0:T(8,128)(2,1)} %collective-permute-done.21.refs_3_), channel_id=1, source_target_pairs={{0,2},{2,0},{1,3},{3,1},{4,6},{6,4},{5,7},{7,5},{8,10},{10,8},{9,1... | collective-permute-start | bytes 786440 | tf_op jit(solution)/shard_map/ppermute | solution.py:210
  70.2 2.7 %collective-permute-done.28.refs_10_ = bf16[128,1024]{1,0:T(8,128)(2,1)S(1)} collective-permute-done((bf16[128,1024]{1,0:T(8,128)(2,1)S(1)}, bf16[128,1024]{1,0:T(8,128)(2,1)S(1)}, u32[]{:S(2)}, u32[]{:S(2)}) %collective-permute-start.28) | collective-permute-done | bytes 262176 | tf_op jit(solution)/shard_map/ppermute | solution.py:210
  74.5 4.1 %collective-permute-done.31.refs_13_ = bf16[128,1024]{1,0:T(8,128)(2,1)S(1)} collective-permute-done((bf16[128,1024]{1,0:T(8,128)(2,1)S(1)}, bf16[128,1024]{1,0:T(8,128)(2,1)S(1)}, u32[]{:S(2)}, u32[]{:S(2)}) %collective-permute-start.31) | collective-permute-done | bytes 262176 | tf_op jit(solution)/shard_map/ppermute | solution.py:210
  79.3 2.1 %collective-permute-start.33 = (bf16[128,1024]{1,0:T(8,128)(2,1)S(1)}, bf16[128,1024]{1,0:T(8,128)(2,1)}, u32[]{:S(2)}, u32[]{:S(2)}) collective-permute-start(bf16[128,1024]{1,0:T(8,128)(2,1)S(1)} %collective-permute-done.24.refs_6_), channel_id=1, source_target_pairs={{0,2},{2,0},{1,3},{3,1},{4,6},{6,4},{5,7},{7,5},{8,10},{10,8},{9,1... | collective-permute-start | bytes 786440 | tf_op jit(solution)/shard_map/ppermute | solution.py:210
  81.4 1.4 collective-permute-start.32
  84.3 6.1 %unpack.2.own_ref = bf16[8,1024,128]{2,1,0:T(8,128)(2,1)} custom-call(s32[256]{0:T(256)} %reshape_reshape.6.flags, bf16[8,432,128]{2,1,0:T(8,128)(2,1)} %all-to-all-done.4.x_ref), custom_call_target="tpu_custom_call" | custom-call | tf_op jit(solution)/shard_map/unpack/pallas_call | solution.py:102
  90.3 2.2 %collective-permute-start.35 = (bf16[64,1024]{1,0:T(8,128)(2,1)S(1)}, bf16[64,1024]{1,0:T(8,128)(2,1)}, u32[]{:S(2)}, u32[]{:S(2)}) collective-permute-start(bf16[64,1024]{1,0:T(8,128)(2,1)S(1)} %collective-permute-done.26.refs_8_), channel_id=1, source_target_pairs={{0,2},{2,0},{1,3},{3,1},{4,6},{6,4},{5,7},{7,5},{8,10},{10,8},{9,1... | collective-permute-start | bytes 393224 | tf_op jit(solution)/shard_map/ppermute | solution.py:210
  92.6 1.4 collective-permute-start.34
  95.4 1.6 reshape_reshape.7.flags
  96.9 6.1 %unpack.3.other_ref = bf16[8,1024,128]{2,1,0:T(8,128)(2,1)} custom-call(s32[256]{0:T(256)} %reshape_reshape.7.flags, bf16[8,432,128]{2,1,0:T(8,128)(2,1)} %collective-permute-done.18.x_ref), custom_call_target="tpu_custom_call" | custom-call | tf_op jit(solution)/shard_map/unpack/pallas_call | solution.py:102
  103.1 1.6 copy-done.2
  109.4 8.7 %product.3 = s16[8,128,1024]{2,1,0:T(8,128)(2,1)S(1)} custom-call(bf16[8,1024,128]{2,1,0:T(8,128)(2,1)S(1)} %copy-done, bf16[8,1024,128]{2,1,0:T(8,128)(2,1)S(1)} %copy-done.2, bf16[128,1024]{1,0:T(8,128)(2,1)S(1)} %copy-done.3, bf16[128,1024]{1,0:T(8,128)(2,1)S(1)} %collective-permute-done.19.refs_1_, ...), custom_call_target="tpu_custom_call" | custom-call | flops 4294967296 | bytes 10485760 | tf_op jit(solution)/shard_map/product/pallas_call | solution.py:163
  119.4 5.9 %all-to-all-start.5 = ((s16[8,128,1024]{2,1,0:T(8,128)(2,1)}), s16[8,128,1024]{2,1,0:T(8,128)(2,1)}, u32[]{:S(2)}, u32[]{:S(2)}) async-start(s16[8,128,1024]{2,1,0:T(8,128)(2,1)} %copy-done.1), calls=%async_computation.5 | async-start | bytes 4194304 | tf_op jit(solution)/shard_map/all_to_all | solution.py:215
  130.2 17.4 %all-to-all-done.5.q_ref = s16[8,128,1024]{2,1,0:T(8,128)(2,1)} async-done(((s16[8,128,1024]{2,1,0:T(8,128)(2,1)}), s16[8,128,1024]{2,1,0:T(8,128)(2,1)}, u32[]{:S(2)}, u32[]{:S(2)}) %all-to-all-start.5) | async-done | bytes 2097184 | tf_op jit(solution)/shard_map/all_to_all | solution.py:215
  147.6 3.9 %squares.3 = (f32[128,1024]{1,0:T(8,128)S(1)}, f32[1,1024]{1,0:T(1,128)}) custom-call(f32[1]{0:T(128)} %bitcast.3.bad, s16[8,128,1024]{2,1,0:T(8,128)(2,1)} %all-to-all-done.5.q_ref), custom_call_target="tpu_custom_call" | custom-call | tf_op jit(solution)/shard_map/squares/pallas_call | solution.py:189
  152.3 12.3 %all_to_all.40 = f32[16,1,1024]{2,1,0:T(1,128)S(1)} all-to-all(f32[16,1,1024]{2,1,0:T(1,128)S(1)} %broadcast_in_dim.13), channel_id=1, replica_groups=mesh['z'=8,'y'=4,'xl'=2,'xh'=2,'core'=2] {'y','xl','xh'}, dimensions={0} | all-to-all | bytes 131072 | tf_op jit(solution)/shard_map/all_to_all | solution.py:218
  165.3 6.9 %all-to-all-start.7 = ((f32[8,1,1024]{2,1,0:T(1,128)}), f32[8,1,1024]{2,1,0:T(1,128)S(1)}, u32[]{:S(2)}, u32[]{:S(2)}) async-start(f32[8,1,1024]{2,1,0:T(1,128)} %broadcast_in_dim.14), calls=%async_computation.7 | async-start | bytes 65536 | tf_op jit(solution)/shard_map/all_to_all | solution.py:218
  172.2 8.0 %all-to-all-done.7 = f32[8,1,1024]{2,1,0:T(1,128)S(1)} async-done(((f32[8,1,1024]{2,1,0:T(1,128)}), f32[8,1,1024]{2,1,0:T(1,128)S(1)}, u32[]{:S(2)}, u32[]{:S(2)}) %all-to-all-start.7) | async-done | bytes 32800 | tf_op jit(solution)/shard_map/all_to_all | solution.py:218
  (79 shorter events, 23.4 us)
Async XLA Ops:
  2.8 15.3 %copy-start.16 = (bf16[128,1024]{1,0:T(8,128)(2,1)S(1)}, bf16[128,1024]{1,0:T(8,128)(2,1)}, u32[]{:S(2)}) copy-start(bf16[128,1024]{1,0:T(8,128)(2,1)} %x_ref.3) | copy-start | bytes 786436
  2.8 15.3 %copy-start.20 = (s32[2,16]{1,0:T(2,128)S(1)}, s32[2,16]{1,0:T(2,128)}, u32[]{:S(2)}) copy-start(s32[2,16]{1,0:T(2,128)} %tiles.2) | copy-start | bytes 388
  9.7 36.9 %all-to-all-start.4 = ((bf16[8,432,128]{2,1,0:T(8,128)(2,1)}), bf16[8,432,128]{2,1,0:T(8,128)(2,1)}, u32[]{:S(2)}, u32[]{:S(2)}) async-start(bf16[8,432,128]{2,1,0:T(8,128)(2,1)} %pack.1), calls=%async_computation.4 | async-start | bytes 1769472 | tf_op jit(solution)/shard_map/all_to_all | solution.py:240
  19.5 25.6 %collective-permute-start.20 = (bf16[128,1024]{1,0:T(8,128)(2,1)}, bf16[128,1024]{1,0:T(8,128)(2,1)S(1)}, u32[]{:S(2)}, u32[]{:S(2)}) collective-permute-start(bf16[128,1024]{1,0:T(8,128)(2,1)} %mask.5.refs_0_), channel_id=1, source_target_pairs={{0,224},{32,0},{64,32},{96,64},{128,96},{160,128},{192,160},{224,1... | collective-permute-start | bytes 786440 | tf_op jit(solution)/shard_map/ppermute | solution.py:205
  22.7 23.9 %collective-permute-start.19 = (bf16[128,1024]{1,0:T(8,128)(2,1)}, bf16[128,1024]{1,0:T(8,128)(2,1)S(1)}, u32[]{:S(2)}, u32[]{:S(2)}) collective-permute-start(bf16[128,1024]{1,0:T(8,128)(2,1)} %mask.5.refs_0_), channel_id=1, source_target_pairs={{0,32},{32,64},{64,96},{96,128},{128,160},{160,192},{192,224},{224... | collective-permute-start | bytes 786440 | tf_op jit(solution)/shard_map/ppermute | solution.py:205
  45.1 6.9 %collective-permute-start.22 = (bf16[128,1024]{1,0:T(8,128)(2,1)S(1)}, bf16[128,1024]{1,0:T(8,128)(2,1)S(1)}, u32[]{:S(2)}, u32[]{:S(2)}) collective-permute-start(bf16[128,1024]{1,0:T(8,128)(2,1)S(1)} %collective-permute-done.20.refs_2_), channel_id=1, source_target_pairs={{0,224},{32,0},{64,32},{96,64},{128,96},{160,128},{192,160},{224,1... | collective-permute-start | bytes 786440 | tf_op jit(solution)/shard_map/ppermute | solution.py:206
  46.5 46.0 %collective-permute-start.18 = (bf16[8,432,128]{2,1,0:T(8,128)(2,1)}, bf16[8,432,128]{2,1,0:T(8,128)(2,1)}, u32[]{:S(2)}, u32[]{:S(2)}) collective-permute-start(bf16[8,432,128]{2,1,0:T(8,128)(2,1)} %all-to-all-done.4.x_ref), channel_id=1, source_target_pairs={{0,1},{1,0},{2,3},{3,2},{4,5},{5,4},{6,7},{7,6},{8,9},{9,8},{10,11... | collective-permute-start | bytes 2654216 | tf_op jit(solution)/shard_map/ppermute | solution.py:228
  46.6 10.0 %collective-permute-start.21 = (bf16[128,1024]{1,0:T(8,128)(2,1)S(1)}, bf16[128,1024]{1,0:T(8,128)(2,1)}, u32[]{:S(2)}, u32[]{:S(2)}) collective-permute-start(bf16[128,1024]{1,0:T(8,128)(2,1)S(1)} %collective-permute-done.19.refs_1_), channel_id=1, source_target_pairs={{0,32},{32,64},{64,96},{96,128},{128,160},{160,192},{192,224},{224... | collective-permute-start | bytes 786440 | tf_op jit(solution)/shard_map/ppermute | solution.py:206
  47.2 11.6 %collective-permute-start.27 = (bf16[128,1024]{1,0:T(8,128)(2,1)}, bf16[128,1024]{1,0:T(8,128)(2,1)S(1)}, u32[]{:S(2)}, u32[]{:S(2)}) collective-permute-start(bf16[128,1024]{1,0:T(8,128)(2,1)} %mask.5.refs_0_), channel_id=1, source_target_pairs={{0,2},{2,0},{1,3},{3,1},{4,6},{6,4},{5,7},{7,5},{8,10},{10,8},{9,1... | collective-permute-start | bytes 786440 | tf_op jit(solution)/shard_map/ppermute | solution.py:210
  51.9 32.4 %copy-start.5 = (bf16[128,1024]{1,0:T(8,128)(2,1)}, bf16[128,1024]{1,0:T(8,128)(2,1)S(1)}, u32[]{:S(2)}) copy-start(bf16[128,1024]{1,0:T(8,128)(2,1)S(1)} %collective-permute-done.22.refs_4_) | copy-start | bytes 786436
  51.9 8.2 %collective-permute-start.24 = (bf16[128,1024]{1,0:T(8,128)(2,1)S(1)}, bf16[128,1024]{1,0:T(8,128)(2,1)S(1)}, u32[]{:S(2)}, u32[]{:S(2)}) collective-permute-start(bf16[128,1024]{1,0:T(8,128)(2,1)S(1)} %collective-permute-done.22.refs_4_), channel_id=1, source_target_pairs={{0,224},{32,0},{64,32},{96,64},{128,96},{160,128},{192,160},{224,1... | collective-permute-start | bytes 786440 | tf_op jit(solution)/shard_map/ppermute | solution.py:207
  56.6 9.3 %collective-permute-start.23 = (bf16[128,1024]{1,0:T(8,128)(2,1)}, bf16[128,1024]{1,0:T(8,128)(2,1)S(1)}, u32[]{:S(2)}, u32[]{:S(2)}) collective-permute-start(bf16[128,1024]{1,0:T(8,128)(2,1)} %collective-permute-done.21.refs_3_), channel_id=1, source_target_pairs={{0,32},{32,64},{64,96},{96,128},{128,160},{160,192},{192,224},{224... | collective-permute-start | bytes 786440 | tf_op jit(solution)/shard_map/ppermute | solution.py:207
  56.6 10.7 %collective-permute-start.29 = (bf16[128,1024]{1,0:T(8,128)(2,1)S(1)}, bf16[128,1024]{1,0:T(8,128)(2,1)S(1)}, u32[]{:S(2)}, u32[]{:S(2)}) collective-permute-start(bf16[128,1024]{1,0:T(8,128)(2,1)S(1)} %collective-permute-done.20.refs_2_), channel_id=1, source_target_pairs={{0,2},{2,0},{1,3},{3,1},{4,6},{6,4},{5,7},{7,5},{8,10},{10,8},{9,1... | collective-permute-start | bytes 786440 | tf_op jit(solution)/shard_map/ppermute | solution.py:210
  58.7 25.5 %copy-start.7 = (bf16[128,1024]{1,0:T(8,128)(2,1)}, bf16[128,1024]{1,0:T(8,128)(2,1)S(1)}, u32[]{:S(2)}) copy-start(bf16[128,1024]{1,0:T(8,128)(2,1)S(1)} %collective-permute-done.27.refs_9_) | copy-start | bytes 786436
  58.7 14.2 %collective-permute-start.28 = (bf16[128,1024]{1,0:T(8,128)(2,1)S(1)}, bf16[128,1024]{1,0:T(8,128)(2,1)S(1)}, u32[]{:S(2)}, u32[]{:S(2)}) collective-permute-start(bf16[128,1024]{1,0:T(8,128)(2,1)S(1)} %collective-permute-done.19.refs_1_), channel_id=1, source_target_pairs={{0,2},{2,0},{1,3},{3,1},{4,6},{6,4},{5,7},{7,5},{8,10},{10,8},{9,1... | collective-permute-start | bytes 786440 | tf_op jit(solution)/shard_map/ppermute | solution.py:210
  60.1 18.4 %collective-permute-start.31 = (bf16[128,1024]{1,0:T(8,128)(2,1)S(1)}, bf16[128,1024]{1,0:T(8,128)(2,1)S(1)}, u32[]{:S(2)}, u32[]{:S(2)}) collective-permute-start(bf16[128,1024]{1,0:T(8,128)(2,1)S(1)} %collective-permute-done.22.refs_4_), channel_id=1, source_target_pairs={{0,2},{2,0},{1,3},{3,1},{4,6},{6,4},{5,7},{7,5},{8,10},{10,8},{9,1... | collective-permute-start | bytes 786440 | tf_op jit(solution)/shard_map/ppermute | solution.py:210
  65.9 15.5 %collective-permute-start.26 = (bf16[64,1024]{1,0:T(8,128)(2,1)S(1)}, bf16[64,1024]{1,0:T(8,128)(2,1)S(1)}, u32[]{:S(2)}, u32[]{:S(2)}) collective-permute-start(bf16[64,1024]{1,0:T(8,128)(2,1)S(1)} %slice.31), channel_id=1, source_target_pairs={{0,224},{32,0},{64,32},{96,64},{128,96},{160,128},{192,160},{224,1... | collective-permute-start | bytes 393224 | tf_op jit(solution)/shard_map/ppermute | solution.py:208
  68.1 34.9 %collective-permute-start.30 = (bf16[128,1024]{1,0:T(8,128)(2,1)}, bf16[128,1024]{1,0:T(8,128)(2,1)}, u32[]{:S(2)}, u32[]{:S(2)}) collective-permute-start(bf16[128,1024]{1,0:T(8,128)(2,1)} %collective-permute-done.21.refs_3_), channel_id=1, source_target_pairs={{0,2},{2,0},{1,3},{3,1},{4,6},{6,4},{5,7},{7,5},{8,10},{10,8},{9,1... | collective-permute-start | bytes 786440 | tf_op jit(solution)/shard_map/ppermute | solution.py:210
  73.7 16.7 %collective-permute-start.25 = (bf16[64,1024]{1,0:T(8,128)(2,1)}, bf16[64,1024]{1,0:T(8,128)(2,1)}, u32[]{:S(2)}, u32[]{:S(2)}) collective-permute-start(bf16[64,1024]{1,0:T(8,128)(2,1)} %slice.30), channel_id=1, source_target_pairs={{0,32},{32,64},{64,96},{96,128},{128,160},{160,192},{192,224},{224... | collective-permute-start | bytes 393224 | tf_op jit(solution)/shard_map/ppermute | solution.py:208
  79.3 23.7 %collective-permute-start.33 = (bf16[128,1024]{1,0:T(8,128)(2,1)S(1)}, bf16[128,1024]{1,0:T(8,128)(2,1)}, u32[]{:S(2)}, u32[]{:S(2)}) collective-permute-start(bf16[128,1024]{1,0:T(8,128)(2,1)S(1)} %collective-permute-done.24.refs_6_), channel_id=1, source_target_pairs={{0,2},{2,0},{1,3},{3,1},{4,6},{6,4},{5,7},{7,5},{8,10},{10,8},{9,1... | collective-permute-start | bytes 786440 | tf_op jit(solution)/shard_map/ppermute | solution.py:210
  81.4 21.6 %collective-permute-start.32 = (bf16[128,1024]{1,0:T(8,128)(2,1)S(1)}, bf16[128,1024]{1,0:T(8,128)(2,1)}, u32[]{:S(2)}, u32[]{:S(2)}) collective-permute-start(bf16[128,1024]{1,0:T(8,128)(2,1)S(1)} %collective-permute-done.23.refs_5_), channel_id=1, source_target_pairs={{0,2},{2,0},{1,3},{3,1},{4,6},{6,4},{5,7},{7,5},{8,10},{10,8},{9,1... | collective-permute-start | bytes 786440 | tf_op jit(solution)/shard_map/ppermute | solution.py:210
  90.3 12.7 %copy-start = (bf16[8,1024,128]{2,1,0:T(8,128)(2,1)S(1)}, bf16[8,1024,128]{2,1,0:T(8,128)(2,1)}, u32[]{:S(2)}) copy-start(bf16[8,1024,128]{2,1,0:T(8,128)(2,1)} %unpack.2.own_ref) | copy-start | bytes 6291460
  90.3 12.7 %copy-start.3 = (bf16[128,1024]{1,0:T(8,128)(2,1)S(1)}, bf16[128,1024]{1,0:T(8,128)(2,1)}, u32[]{:S(2)}) copy-start(bf16[128,1024]{1,0:T(8,128)(2,1)} %mask.5.refs_0_) | copy-start | bytes 786436
  90.3 12.7 %collective-permute-start.35 = (bf16[64,1024]{1,0:T(8,128)(2,1)S(1)}, bf16[64,1024]{1,0:T(8,128)(2,1)}, u32[]{:S(2)}, u32[]{:S(2)}) collective-permute-start(bf16[64,1024]{1,0:T(8,128)(2,1)S(1)} %collective-permute-done.26.refs_8_), channel_id=1, source_target_pairs={{0,2},{2,0},{1,3},{3,1},{4,6},{6,4},{5,7},{7,5},{8,10},{10,8},{9,1... | collective-permute-start | bytes 393224 | tf_op jit(solution)/shard_map/ppermute | solution.py:210
  92.6 10.4 %collective-permute-start.34 = (bf16[64,1024]{1,0:T(8,128)(2,1)}, bf16[64,1024]{1,0:T(8,128)(2,1)}, u32[]{:S(2)}, u32[]{:S(2)}) collective-permute-start(bf16[64,1024]{1,0:T(8,128)(2,1)} %collective-permute-done.25.refs_7_), channel_id=1, source_target_pairs={{0,2},{2,0},{1,3},{3,1},{4,6},{6,4},{5,7},{7,5},{8,10},{10,8},{9,1... | collective-permute-start | bytes 393224 | tf_op jit(solution)/shard_map/ppermute | solution.py:210
  103.0 1.6 copy-start.2
  118.1 1.3 copy-start.1
  119.4 28.2 %all-to-all-start.5 = ((s16[8,128,1024]{2,1,0:T(8,128)(2,1)}), s16[8,128,1024]{2,1,0:T(8,128)(2,1)}, u32[]{:S(2)}, u32[]{:S(2)}) async-start(s16[8,128,1024]{2,1,0:T(8,128)(2,1)} %copy-done.1), calls=%async_computation.5 | async-start | bytes 4194304 | tf_op jit(solution)/shard_map/all_to_all | solution.py:215
  125.3 56.1 %copy-start.15 = (bf16[8192,128]{1,0:T(8,128)(2,1)S(1)}, bf16[8192,128]{1,0:T(8,128)(2,1)}, u32[]{:S(2)}) copy-start(bf16[8192,128]{1,0:T(8,128)(2,1)} %x_ref.2) | copy-start | bytes 6291460
  125.3 56.1 %copy-start.17 = (bf16[128,1024]{1,0:T(8,128)(2,1)S(1)}, bf16[128,1024]{1,0:T(8,128)(2,1)}, u32[]{:S(2)}) copy-start(bf16[128,1024]{1,0:T(8,128)(2,1)} %x_ref.3) | copy-start | bytes 786436
  125.3 56.1 %copy-start.19 = (s32[128,2]{0,1:T(2,128)S(1)}, s32[128,2]{0,1:T(2,128)}, u32[]{:S(2)}) copy-start(s32[128,2]{0,1:T(2,128)} %param.7) | copy-start | bytes 3076
  165.3 15.0 %all-to-all-start.7 = ((f32[8,1,1024]{2,1,0:T(1,128)}), f32[8,1,1024]{2,1,0:T(1,128)S(1)}, u32[]{:S(2)}, u32[]{:S(2)}) async-start(f32[8,1,1024]{2,1,0:T(1,128)} %broadcast_in_dim.14), calls=%async_computation.7 | async-start | bytes 65536 | tf_op jit(solution)/shard_map/all_to_all | solution.py:218
  (9 other events, 7.7 us)
